TPU v7x, 256 devices: a whole 4x4x8 slice. The times are simulated.
256 devices in a mesh: pair: 32 (over z_lo, x, y), virt: 8 (over z_hi, core).
Axes of the slice: x: 4, y: 4, z: 8 (z_hi: 4, z_lo: 2; z = z_hi * 2 + z_lo), core: 2. Of those that a mesh axis runs over, the one named last changes fastest.
Arguments:
- amplitudes: float32 [32, 2048, 2048], P('pair', 'virt'), may hold values from -6 to 6
- integrals: float32 [32, 2048, 2048], P('pair', 'virt'), may hold values from -12 to 12
- operator: float32 [2048, 2048], P('virt'), may hold values from -0.375 to 0.375
- virt_energy: float32 [2048], replicated, may hold values from 0.5 to 2.5
- pair_energy: float32 [32], P('pair'), may hold values from 1 to 3
- block_mask: int32 [16, 16], replicated, may hold values from 0 to 1, as said below
- partner: int32 [32], replicated, may hold values from 0 to 31, as said below
Outputs:
- updated: float32 [32, 2048, 2048], P('pair', 'virt')
Inputs may be any that keep to these rules, and one draw needn't show every extreme that they name: `block_mask`: each block row holds 2 to 10 present blocks; some block row holds exactly 10. partner[partner[p]] = p and partner[p] != p for every pair p.
All inputs are finite; a program needn't handle non-finite values.
Results may differ from a plain program's by a relative error of at most 0.0001.
Values sent between devices are 32-bit elements; how exact they have to be, the bound alone decides.
A program may use at most 128 MiB of HBM per device.

v0:
```python
import jax
import jax.numpy as jnp
from jax import lax
from jax.sharding import PartitionSpec as P

ITERS = 2


def reflect(product):
    moved = lax.all_to_all(product, "virt", split_axis=2, concat_axis=1, tiled=True)
    return jnp.swapaxes(moved, 1, 2)


def reverse_pairs(values, partner):
    pair_count, row_count, width = values.shape
    groups = lax.axis_size("pair")
    slabs = values.reshape(pair_count, groups, row_count // groups, width)
    spread = lax.all_to_all(slabs, "pair", split_axis=1, concat_axis=0, tiled=True)
    turned = jnp.take(spread, partner, axis=0)
    returned = lax.all_to_all(turned, "pair", split_axis=0, concat_axis=1, tiled=True)
    return returned.reshape(pair_count, row_count, width)


def per_device(amplitudes, integrals, operator, virt_energy, pair_energy, block_mask, partner):
    pair_count, row_count, width = amplitudes.shape
    block_count = block_mask.shape[0]
    block_size = width // block_count
    gathered = lax.all_gather(operator, "virt", axis=0, tiled=True)
    mask_values = block_mask.astype(jnp.float32)
    masked = (
        gathered.reshape(block_count, block_size, block_count, block_size)
        * mask_values[:, None, :, None]
    ).reshape(width, width)
    row_start = lax.axis_index("virt") * row_count
    own_energy = lax.dynamic_slice_in_dim(virt_energy, row_start, row_count)
    denominator = (
        own_energy[None, :, None] + virt_energy[None, None, :] + pair_energy[:, None, None]
    )
    current = amplitudes
    for sweep in range(ITERS):
        product = jnp.einsum("prc,cb->prb", current, masked, precision=lax.Precision.HIGHEST)
        mirror = reverse_pairs(reflect(product), partner)
        current = (integrals + product + mirror) / denominator
    return current


def solution(mesh):
    return jax.shard_map(
        per_device,
        mesh=mesh,
        in_specs=(
            P("pair", "virt", None),
            P("pair", "virt", None),
            P("virt", None),
            P(),
            P("pair"),
            P(),
            P(),
        ),
        out_specs=P("pair", "virt", None),
        check_vma=False,
    )
```

profile of v0, /device:TPU:30, one launch (start us, length us, event | category | flops | bytes accessed | tf_op | source)
XLA Modules:
  0.0 542.7 jit_solution(14309356418793888707)
XLA Ops:
  6.5 0.0 copy-start
  6.5 0.0 copy-start.6
  6.5 0.0 all-gather.2.cloned.1.call-start
  6.5 0.7 all-gather.2.cloned.1.call-update
  7.3 0.1 copy-done.6
  7.4 161.7 %all-gather.2.cloned.1.call-done = f32[2048,2048]{1,0:T(8,128)} async-done(((f32[256,2048]{1,0:T(8,128)}), f32[2048,2048]{1,0:T(8,128)}) %all-gather.2.cloned.1.call-update) | async-done | bytes 16777232 | tf_op jit(solution)/shard_map/all_gather | solution.py:28
  169.1 6.9 %mul.14 = f32[16,128,16,128]{3,2,1,0:T(8,128)} broadcast(f32[16,16]{1,0:T(8,128)S(1)} %convert_element_type.3), dimensions={0,2} | broadcast | bytes 16778240 | tf_op jit(solution)/shard_map/mul | solution.py:31
  175.9 0.0 copy-done
  175.9 36.4 %fusion.2 = f32[1,256,2048]{1,2,0:T(8,128)S(1)} fusion(f32[2048,2048]{1,0:T(8,128)} %all-gather.2.cloned.1.call-done, f32[256,8,16,128]{3,2,1,0:T(8,128)} %bitcast.61, f32[1,256,2048]{2,1,0:T(8,128)S(1)} %copy-done), kind=kOutput, calls=%fused_computation.5 | convolution fusion | flops 12889096192 | bytes 37748736 | tf_op jit(solution)/shard_map/prc,cb->prb/dot_general | solution.py:41
  212.3 0.0 copy-start.2
  212.3 8.6 %copy.37 = f32[1,256,2048]{1,0,2:T(1,128)S(1)} copy(f32[1,256,2048]{1,2,0:T(8,128)S(1)} %fusion.2) | data formatting | bytes 4194304 | tf_op jit(solution)/shard_map/prc,cb->prb/dot_general | solution.py:41
  220.9 0.0 copy-done.2
  220.9 55.0 %all_to_all.78 = f32[1,256,2048]{1,0,2:T(1,128)S(1)} all-to-all(f32[1,256,2048]{1,0,2:T(1,128)S(1)} %copy.37), channel_id=1, replica_groups=mesh['pair'=32,'virt'=8] {'virt'}, dimensions={2} | all-to-all | bytes 4194304 | tf_op jit(solution)/shard_map/all_to_all | solution.py:10
  276.0 1.5 copy.53
  277.4 1.9 copy.38
  279.3 1.8 copy.39
  281.1 0.0 copy-start.7
  281.2 8.3 %all-to-all-start.1 = ((f32[1,32,8,2048]{3,2,0,1:T(8,128)}), f32[1,32,8,2048]{3,2,0,1:T(8,128)S(1)}, u32[]{:S(2)}, u32[]{:S(2)}) async-start(f32[1,32,8,2048]{3,2,0,1:T(8,128)} %bitcast.65), calls=%async_computation.1 | async-start | bytes 4194304 | tf_op jit(solution)/shard_map/all_to_all | solution.py:18
  289.4 0.0 copy-done.7
  289.5 25.4 %all-to-all-done.1 = f32[1,32,8,2048]{3,2,0,1:T(8,128)S(1)} async-done(((f32[1,32,8,2048]{3,2,0,1:T(8,128)}), f32[1,32,8,2048]{3,2,0,1:T(8,128)S(1)}, u32[]{:S(2)}, u32[]{:S(2)}) %all-to-all-start.1) | async-done | bytes 2097184 | tf_op jit(solution)/shard_map/all_to_all | solution.py:18
  314.9 2.0 gather_fusion
  316.9 3.1 fusion.6
  320.0 7.9 %all-to-all-start.2 = ((f32[32,1,8,2048]{3,2,1,0:T(8,128)}), f32[32,1,8,2048]{3,2,1,0:T(8,128)S(1)}, u32[]{:S(2)}, u32[]{:S(2)}) async-start(f32[32,1,8,2048]{3,2,1,0:T(8,128)} %fusion.6), calls=%async_computation.2 | async-start | bytes 4194304 | tf_op jit(solution)/shard_map/all_to_all | solution.py:20
  328.0 0.0 copy-start.5
  328.0 2.9 copy.44
  331.6 0.0 copy-done.5
  331.6 0.1 dynamic_slice.3
  331.6 22.1 %all-to-all-done.2 = f32[32,1,8,2048]{3,2,1,0:T(8,128)S(1)} async-done(((f32[32,1,8,2048]{3,2,1,0:T(8,128)}), f32[32,1,8,2048]{3,2,1,0:T(8,128)S(1)}, u32[]{:S(2)}, u32[]{:S(2)}) %all-to-all-start.2) | async-done | bytes 2097184 | tf_op jit(solution)/shard_map/all_to_all | solution.py:20
  353.7 0.0 copy-start.4
  353.7 1.3 copy-done.4
  355.1 0.0 copy-start.3
  355.1 3.1 copy.42
  358.2 0.0 copy-done.3
  358.2 37.5 %fusion.3 = f32[1,256,2048]{1,2,0:T(8,128)} fusion(f32[2048,2048]{1,0:T(8,128)} %all-gather.2.cloned.1.call-done, f32[256,8,16,128]{3,2,1,0:T(8,128)} %bitcast.62, f32[1,256,2048]{1,2,0:T(8,128)} %copy.42, f32[1,256,2048]{1,2,0:T(8,128)} %copy.44, f32[1,256,2048]{1,2,0:T(8,128)S(1)} %copy-done.3, f32[]{:T(128)} %bitcast.59, f32[2048]{0:T(1024)S(1)} %copy-done.5, ...), kind=kOutput, calls=%fused_computation.6 | convolution fusion | flops 12891717632 | bytes 41952260 | tf_op jit(solution)/shard_map/prc,cb->prb/dot_general | solution.py:41
  395.7 3.8 copy.45
  399.5 54.6 %all_to_all.79 = f32[1,256,2048]{1,0,2:T(1,128)S(1)} all-to-all(f32[1,256,2048]{1,0,2:T(1,128)S(1)} %copy.45), channel_id=1, replica_groups=mesh['pair'=32,'virt'=8] {'virt'}, dimensions={2} | all-to-all | bytes 4194304 | tf_op jit(solution)/shard_map/all_to_all | solution.py:10
  454.0 1.5 copy.54
  455.5 1.9 copy.46
  457.4 1.8 copy.47
  459.3 32.9 %all_to_all.80 = f32[1,32,8,2048]{3,2,0,1:T(8,128)} all-to-all(f32[1,32,8,2048]{3,2,0,1:T(8,128)} %bitcast.71), channel_id=1, replica_groups=mesh['pair'=32,'virt'=8] {'pair'}, dimensions={1} | all-to-all | bytes 4194304 | tf_op jit(solution)/shard_map/all_to_all | solution.py:18
  492.1 2.3 gather_fusion.1
  494.4 0.2 fusion.4
  494.6 31.8 %all_to_all.81 = f32[32,1,8,2048]{3,2,1,0:T(8,128)S(1)} all-to-all(f32[32,1,8,2048]{3,2,1,0:T(8,128)S(1)} %fusion.4), channel_id=1, replica_groups=mesh['pair'=32,'virt'=8] {'pair'}, dimensions={0} | all-to-all | bytes 4194304 | tf_op jit(solution)/shard_map/all_to_all | solution.py:20
  526.4 1.8 copy.50
  528.2 0.0 copy-start.1
  528.2 4.8 add_divide_fusion
  533.0 2.9 copy.51
  535.9 0.0 copy-done.1
  (4 shorter events, 0.0 us)
Async XLA Ops:
  6.5 169.4 %copy-start = (f32[1,256,2048]{2,1,0:T(8,128)S(1)}, f32[1,256,2048]{2,1,0:T(8,128)}, u32[]{:S(2)}) copy-start(f32[1,256,2048]{2,1,0:T(8,128)} %param.9) | copy-start | bytes 6291460
  6.5 0.8 copy-start.6
  6.5 162.5 %all-gather.2.cloned.1.call-start = ((), (), s32[]{:S(2)}) async-start(), calls=%async_computation.6 | async-start | bytes 18874368 | tf_op jit(solution)/shard_map/all_gather | solution.py:28
  212.3 8.6 %copy-start.2 = (f32[1,256,2048]{1,2,0:T(8,128)}, f32[1,256,2048]{1,2,0:T(8,128)S(1)}, u32[]{:S(2)}) copy-start(f32[1,256,2048]{1,2,0:T(8,128)S(1)} %fusion.2) | copy-start | bytes 6291460
  281.1 8.3 %copy-start.7 = (s32[32]{0:T(128)S(1)}, s32[32]{0:T(128)}, u32[]{:S(2)}) copy-start(s32[32]{0:T(128)} %param.15) | copy-start | bytes 388
  281.2 33.8 %all-to-all-start.1 = ((f32[1,32,8,2048]{3,2,0,1:T(8,128)}), f32[1,32,8,2048]{3,2,0,1:T(8,128)S(1)}, u32[]{:S(2)}, u32[]{:S(2)}) async-start(f32[1,32,8,2048]{3,2,0,1:T(8,128)} %bitcast.65), calls=%async_computation.1 | async-start | bytes 4194304 | tf_op jit(solution)/shard_map/all_to_all | solution.py:18
  320.0 33.7 %all-to-all-start.2 = ((f32[32,1,8,2048]{3,2,1,0:T(8,128)}), f32[32,1,8,2048]{3,2,1,0:T(8,128)S(1)}, u32[]{:S(2)}, u32[]{:S(2)}) async-start(f32[32,1,8,2048]{3,2,1,0:T(8,128)} %fusion.6), calls=%async_computation.2 | async-start | bytes 4194304 | tf_op jit(solution)/shard_map/all_to_all | solution.py:20
  328.0 3.6 copy-start.5
  353.7 1.3 copy-start.4
  355.1 3.1 copy-start.3
  528.2 7.7 %copy-start.1 = (f32[1,256,2048]{2,1,0:T(8,128)S(1)}, f32[1,256,2048]{2,1,0:T(8,128)}, u32[]{:S(2)}) copy-start(f32[1,256,2048]{2,1,0:T(8,128)} %param.9) | copy-start | bytes 6291460
Sparse Core Ops, SparseCore 0:
  9.2 159.7 all-gather.1
where the time goes:
time: 546 us; the launch traced here: 543 us
  waiting for transfers between devices  210 us (38%)
  blocking collectives  174 us (32%)
  matrix products  73.9 us (14%)
  local copies, waits for them, and re-layouts  46.2 us (8%)
  starting transfers between devices  16.2 us (3%)
  between operations  14.2 us (3%)
  other arithmetic  8.15 us (1%)
    all_gather x1, waiting for transfers between devices, per_device(): gathered = lax.all_gather(operator, 'virt', axis=0, tiled=True)  162 us
    all_to_all x2, blocking collectives, reflect(): lax.all_to_all(product, 'virt', split_axis=2, concat_axis=1, tiled=True)  110 us
    dot_general x2, matrix products, per_device(): jnp.einsum('prc,cb->prb', current, masked, precision=lax.Precision.HIGHEST)  73.9 us
    all_to_all x1, blocking collectives, reverse_pairs(): lax.all_to_all(slabs, 'pair', split_axis=1, concat_axis=0, tiled=True)  32.9 us
    all_to_all x1, blocking collectives, reverse_pairs(): lax.all_to_all(turned, 'pair', split_axis=0, concat_axis=1, tiled=True)  31.8 us
    all_to_all x1, waiting for transfers between devices, reverse_pairs(): lax.all_to_all(slabs, 'pair', split_axis=1, concat_axis=0, tiled=True)  25.4 us
    all_to_all x1, waiting for transfers between devices, reverse_pairs(): lax.all_to_all(turned, 'pair', split_axis=0, concat_axis=1, tiled=True)  22.1 us
    dot_general x2, local copies, waits for them, and re-layouts, per_device(): jnp.einsum('prc,cb->prb', current, masked, precision=lax.Precision.HIGHEST)  12.3 us
  transfers between devices with their start and end apart: 3, of which 3 were waited for; matrix products, arithmetic and copies ran while one was open for 1% of the time, Pallas kernels for 0%

commit v1 on v0

v1 whole, which is shorter than its diff:
```python
import jax
import jax.numpy as jnp
from jax import lax
from jax.experimental import pallas as pl
from jax.experimental.pallas import tpu as pltpu
from jax.sharding import PartitionSpec as P

ITERS = 2
MESH = pl.DeviceIdType.MESH


def mirror_kernel(
    partner_ref, turned_in, mirror, spread, turned, out1, in1, out2, in2, ready
):
    pairs, virts = lax.axis_size("pair"), lax.axis_size("virt")
    total = pairs * virts
    p, v = lax.axis_index("pair"), lax.axis_index("virt")
    me = p * virts + v
    barrier = pltpu.get_barrier_semaphore()

    def tell(semaphore, axis, mine, count):
        def one(step, carry):
            pl.semaphore_signal(
                semaphore,
                inc=1,
                device_id={axis: lax.rem(mine + step, count)},
                device_id_type=MESH,
            )
            return carry

        lax.fori_loop(1, count, one, 0)

    tell(barrier, "pair", p, pairs)
    tell(barrier, "virt", v, virts)
    pl.semaphore_wait(barrier, pairs + virts - 2)
    tell(ready, "virt", v, virts)
    pl.semaphore_wait(ready, virts - 1)

    width = turned_in.shape[2]
    place = pl.ds(pl.multiple_of(v * width, width), width)

    def scatter(step, carry):
        target = lax.rem(me + step, total)
        pair, virt = target // virts, lax.rem(target, virts)
        pltpu.make_async_remote_copy(
            src_ref=turned_in.at[virt * pairs + pair],
            dst_ref=spread.at[p, :, place],
            send_sem=out1,
            recv_sem=in1,
            device_id={"pair": pair, "virt": virt},
            device_id_type=MESH,
        ).start()
        return carry

    lax.fori_loop(1, total, scatter, 0)
    pltpu.make_async_copy(
        turned_in.at[v * pairs + p], spread.at[p, :, place], in1
    ).start()
    pltpu.make_async_copy(spread, spread, in1).wait()

    def give(step, carry):
        pair = lax.rem(p + step, pairs)
        turned[pair] = spread[partner_ref[pair]]
        pltpu.make_async_remote_copy(
            src_ref=turned.at[pair],
            dst_ref=mirror.at[p],
            send_sem=out2,
            recv_sem=in2,
            device_id={"pair": pair},
            device_id_type=MESH,
        ).start()
        return carry

    lax.fori_loop(1, pairs, give, 0)
    turned[p] = spread[partner_ref[p]]
    pltpu.make_async_copy(turned.at[p], mirror.at[p], in2).start()
    sent = turned_in.at[pl.ds(0, total - 1)]
    pltpu.make_async_copy(sent, sent, out1).wait()
    pltpu.make_async_copy(mirror, mirror, in2).wait()
    sent = turned.at[pl.ds(0, pairs - 1)]
    pltpu.make_async_copy(sent, sent, out2).wait()


def mirror_of(product, partner):
    rows, width = product.shape
    pairs, virts = lax.axis_size("pair"), lax.axis_size("virt")
    slab = width // (pairs * virts)
    shape = (pairs, slab, width)
    return pl.pallas_call(
        mirror_kernel,
        out_shape=jax.ShapeDtypeStruct(shape, jnp.float32),
        in_specs=[
            pl.BlockSpec(memory_space=pltpu.SMEM),
            pl.BlockSpec(memory_space=pltpu.VMEM),
        ],
        out_specs=pl.BlockSpec(memory_space=pltpu.VMEM),
        scratch_shapes=[pltpu.VMEM(shape, jnp.float32)] * 2
        + [pltpu.SemaphoreType.DMA] * 4
        + [pltpu.SemaphoreType.REGULAR],
        compiler_params=pltpu.CompilerParams(
            collective_id=0, has_side_effects=True, vmem_limit_bytes=24 << 20
        ),
    )(partner, product.T.reshape(pairs * virts, slab, rows)).reshape(rows, width)


def per_device(amplitudes, integrals, operator, virt_energy, pair_energy, block_mask, partner):
    pair_count, row_count, width = amplitudes.shape
    block_count = block_mask.shape[0]
    block_size = width // block_count
    gathered = lax.all_gather(operator, "virt", axis=0, tiled=True)
    mask_values = block_mask.astype(jnp.float32)
    masked = (
        gathered.reshape(block_count, block_size, block_count, block_size)
        * mask_values[:, None, :, None]
    ).reshape(width, width)
    row_start = lax.axis_index("virt") * row_count
    own_energy = lax.dynamic_slice_in_dim(virt_energy, row_start, row_count)
    denominator = own_energy[:, None] + virt_energy[None, :] + pair_energy[0]
    current = amplitudes[0]
    for sweep in range(ITERS):
        product = jnp.dot(current, masked, precision=lax.Precision.HIGH)
        mirror = mirror_of(product, partner)
        current = (integrals[0] + product + mirror) / denominator
    return current[None]


def solution(mesh):
    return jax.shard_map(
        per_device,
        mesh=mesh,
        in_specs=(
            P("pair", "virt", None),
            P("pair", "virt", None),
            P("virt", None),
            P(),
            P("pair"),
            P(),
            P(),
        ),
        out_specs=P("pair", "virt", None),
        check_vma=False,
    )
```

time: 546 us -> 448 us (0.82)
  Pallas kernels: 0 us -> 199 us
  blocking collectives: 174 us -> 0 us
  waiting for transfers between devices: 210 us -> 159 us
  matrix products: 73.9 us -> 42.3 us
  local copies, waits for them, and re-layouts: 46.2 us -> 28.7 us
  starting transfers between devices: 16.2 us -> 0.01 us
    pallas_call x0 -> x2, Pallas kernels: none -> 199 us  [mirror_of(): pl.pallas_call(mirror_kernel, out_shape=jax.ShapeDtypeStruct(shape, jnp.f...]
    all_to_all x4 -> x0, blocking collectives: 174 us -> none  [the longest x2 110 us: reflect(): lax.all_to_all(product, 'virt', split_axis=2, concat_axis=1, tiled=True)]
    all_to_all x2 -> x0, waiting for transfers between devices: 47.5 us -> none  [the longest x1 25.4 us: reverse_pairs(): lax.all_to_all(slabs, 'pair', split_axis=1, concat_axis=0, tiled=True)]
    dot_general x2, matrix products: 73.9 us -> 42.3 us  [per_device(): product = jnp.dot(current, masked, precision=lax.Precision.HIGH)]
    all_to_all x2 -> x0, starting transfers between devices: 16.2 us -> none  [the longest x1 8.28 us: reverse_pairs(): lax.all_to_all(slabs, 'pair', split_axis=1, concat_axis=0, tiled=True)]
    dot_general x2 -> x1, local copies, waits for them, and re-layouts: 12.3 us -> 2.93 us  [per_device(): product = jnp.dot(current, masked, precision=lax.Precision.HIGH)]
  transfers between devices with their start and end apart: 3 -> 1, of which waited for: 3 -> 1; matrix products, arithmetic and copies ran while one was open for 1% -> 1% of each run, Pallas kernels for 0% -> 0%
where the time goes in v1:
time: 448 us
  Pallas kernels  199 us (44%)
  waiting for transfers between devices  159 us (35%)
  matrix products  42.3 us (9%)
  local copies, waits for them, and re-layouts  28.7 us (6%)
  between operations  14.1 us (3%)
  other arithmetic  4.65 us (1%)
    pallas_call x2, Pallas kernels, mirror_of(): pl.pallas_call(mirror_kernel, out_shape=jax.ShapeDtypeStruct(shape, jnp.f...  199 us
    all_gather x1, waiting for transfers between devices, per_device(): gathered = lax.all_gather(operator, 'virt', axis=0, tiled=True)  158 us
    dot_general x2, matrix products, per_device(): product = jnp.dot(current, masked, precision=lax.Precision.HIGH)  42.3 us
  transfers between devices with their start and end apart: 1, of which 1 were waited for; matrix products, arithmetic and copies ran while one was open for 1% of the time, Pallas kernels for 0%

profile of v1, /device:TPU:30, one launch (start us, length us, event | category | flops | bytes accessed | tf_op | source)
XLA Modules:
  0.0 448.0 jit_solution(9629311213448052378)
XLA Ops:
  6.5 0.0 copy-start
  6.5 0.0 copy-start.7
  6.5 0.0 all-gather.2.cloned.1.call-start
  6.5 0.7 all-gather.2.cloned.1.call-update
  7.9 0.0 copy-done.7
  7.9 0.0 copy-start.6
  7.9 2.9 copy.8
  10.9 0.0 copy-done.6
  10.9 0.1 dynamic_slice.3
  11.0 158.1 %all-gather.2.cloned.1.call-done = f32[2048,2048]{1,0:T(8,128)} async-done(((f32[256,2048]{1,0:T(8,128)}), f32[2048,2048]{1,0:T(8,128)}) %all-gather.2.cloned.1.call-update) | async-done | bytes 16777232 | tf_op jit(solution)/shard_map/all_gather | solution.py:110
  169.1 6.9 %mul.14 = f32[16,128,16,128]{3,2,1,0:T(8,128)} broadcast(f32[16,16]{1,0:T(8,128)S(1)} %convert_element_type.3), dimensions={0,2} | broadcast | bytes 16778240 | tf_op jit(solution)/shard_map/mul | solution.py:113
  175.9 0.0 copy-done
  175.9 0.0 copy-start.5
  175.9 21.5 %fusion.1 = f32[2048,256]{1,0:T(8,128)S(1)} fusion(f32[2048,2048]{1,0:T(8,128)} %all-gather.2.cloned.1.call-done, f32[256,8,16,128]{3,2,1,0:T(8,128)} %bitcast.42, f32[1,256,2048]{2,1,0:T(8,128)S(1)} %copy-done), kind=kOutput, calls=%fused_computation.2 | convolution fusion | flops 6446645248 | bytes 37748736 | tf_op jit(solution)/shard_map/dot_general | solution.py:121
  197.4 0.0 copy-start.1
  197.4 0.0 copy-done.5
  197.4 98.0 %shard_map.73 = f32[32,8,2048]{2,1,0:T(8,128)S(1)} custom-call(s32[32]{0:T(128)S(1)} %copy-done.5, f32[256,8,256]{2,1,0:T(8,128)S(1)} %bitcast.38), custom_call_target="tpu_custom_call" | custom-call | tf_op jit(solution)/shard_map/pallas_call | solution.py:89
  295.4 0.0 copy-done.1
  295.4 0.0 copy-start.4
  295.5 1.3 copy-done.4
  296.8 2.9 copy.9
  299.7 20.8 %fusion = f32[256,2048]{1,0:T(8,128)} fusion(f32[2048,2048]{1,0:T(8,128)} %all-gather.2.cloned.1.call-done, f32[256,8,16,128]{3,2,1,0:T(8,128)} %bitcast.43, f32[256,2048]{0,1:T(8,128)} %copy.9, f32[2048,256]{1,0:T(8,128)} %copy-done.1, f32[1,256,2048]{1,2,0:T(8,128)} %copy.8, f32[]{:T(128)} %bitcast.36, f32[2048]{0:T(1024)S(1)} %copy-done.6, ...), kind=kOutput, calls=%fused_computation.1 | convolution fusion | flops 6449266688 | bytes 41952260 | tf_op jit(solution)/shard_map/dot_general | solution.py:121
  320.6 2.9 copy.10
  323.5 2.9 copy.11
  326.4 0.0 copy-start.2
  326.4 1.6 copy-done.2
  328.0 101.4 %shard_map.74 = f32[32,8,2048]{2,1,0:T(8,128)S(1)} custom-call(s32[32]{0:T(128)S(1)} %copy-done.5, f32[256,8,256]{2,1,0:T(8,128)S(1)} %bitcast.39), custom_call_target="tpu_custom_call" | custom-call | tf_op jit(solution)/shard_map/pallas_call | solution.py:89
  429.4 0.0 copy-start.3
  429.4 1.3 copy-done.3
  430.7 2.9 copy.12
  433.6 4.7 %fusion.9 = f32[1,256,2048]{1,2,0:T(8,128)} fusion(f32[256,2048]{0,1:T(8,128)} %copy.12, f32[256,2048]{0,1:T(8,128)} %copy.10, f32[1,256,2048]{1,2,0:T(8,128)} %copy.8, f32[]{:T(128)} %bitcast.37, f32[2048]{0:T(1024)S(1)} %copy-done.6, f32[256]{0:T(256)S(1)} %dynamic_slice.3), kind=kLoop, calls=%fused_computation.11 | loop fusion | flops 2621440 | bytes 8397828 | tf_op jit(solution)/shard_map/broadcast_in_dim | solution.py:124
  438.3 2.9 copy.13
  (1 shorter events, 0.0 us)
Async XLA Ops:
  6.5 169.4 %copy-start = (f32[1,256,2048]{2,1,0:T(8,128)S(1)}, f32[1,256,2048]{2,1,0:T(8,128)}, u32[]{:S(2)}) copy-start(f32[1,256,2048]{2,1,0:T(8,128)} %param.7) | copy-start | bytes 6291460
  6.5 1.4 copy-start.7
  6.5 162.5 %all-gather.2.cloned.1.call-start = ((), (), s32[]{:S(2)}) async-start(), calls=%async_computation | async-start | bytes 18874368 | tf_op jit(solution)/shard_map/all_gather | solution.py:110
  7.9 3.0 copy-start.6
  175.9 21.5 %copy-start.5 = (s32[32]{0:T(128)S(1)}, s32[32]{0:T(128)}, u32[]{:S(2)}) copy-start(s32[32]{0:T(128)} %partner_ref.3) | copy-start | bytes 388
  197.4 98.0 %copy-start.1 = (f32[2048,256]{1,0:T(8,128)}, f32[2048,256]{1,0:T(8,128)S(1)}, u32[]{:S(2)}) copy-start(f32[2048,256]{1,0:T(8,128)S(1)} %fusion.1) | copy-start | bytes 6291460
  295.4 1.3 copy-start.4
  326.4 1.6 copy-start.2
  429.4 1.3 copy-start.3
Sparse Core Ops, SparseCore 0:
  9.2 159.7 all-gather.1

commit v2 on v0

v2 whole, which is shorter than its diff:
```python
import jax
import jax.numpy as jnp
from jax import lax
from jax.experimental import pallas as pl
from jax.experimental.pallas import tpu as pltpu
from jax.sharding import PartitionSpec as P

ITERS = 2
MESH = pl.DeviceIdType.MESH
PAIRS, VIRTS = 32, 8
TOTAL = PAIRS * VIRTS
WIDTH, ROWS, BLOCK, BLOCKS, SLOTS = 2048, 256, 128, 16, 10
HALVES = 2
SLAB = WIDTH // TOTAL
F32, BF16 = jnp.float32, jnp.bfloat16
JS = (1, 3, 2)
KINDS = 10


def split(value):
    high = value.astype(BF16)
    return high, (value - high.astype(F32)).astype(BF16)


def three_dots(a_high, a_low, b_high, b_low):
    def dot(a, b):
        return jnp.dot(a, b, preferred_element_type=F32)

    return dot(a_high, b_high) + (dot(a_high, b_low) + dot(a_low, b_high))


def kernel(
    partner_ref, slot_ref, flag_ref, column_ref, pair_ref, amp_hbm, int_hbm, op_hbm, own_ref, virt_ref,
    out_ref,
    amp, ints, op0, op1, prod, a_high, a_low, w_high, w_low, *rest,
):
    got = [[[rest[(j * 2 + cc) * 2 + h] for h in range(2)] for cc in range(2)] for j in range(4)]
    rest = rest[16:]
    turned_in, spread, turned, mirror = (
        rest[0:2], (rest[2:4], rest[4:6]), rest[6:8], (rest[8:10], rest[10:12])
    )
    load_sem, gather_out, gather_in, hop_out, hop_in, ready = rest[12:]

    p, v = lax.axis_index("pair"), lax.axis_index("virt")
    z_lo, x, y = p // 16, lax.rem(p // 4, 4), lax.rem(p, 4)
    z_hi, core = v // 2, lax.rem(v, 2)
    op = (op0, op1)
    barrier = pltpu.get_barrier_semaphore()

    loads = [
        pltpu.make_async_copy(
            op_hbm.at[pl.ds(h * BLOCK, BLOCK), pl.ds(c * BLOCK, BLOCK)], op[h].at[c], load_sem.at[h]
        )
        for h in range(2) for c in range(BLOCKS)
    ] + [
        pltpu.make_async_copy(amp_hbm, amp, load_sem.at[2]),
        pltpu.make_async_copy(int_hbm, ints, load_sem.at[3]),
    ]
    for load in loads:
        load.start()

    def tell(semaphore, axis, mine, count):
        def one(step, carry):
            pl.semaphore_signal(
                semaphore, inc=1, device_id={axis: lax.rem(mine + step, count)}, device_id_type=MESH
            )
            return carry

        lax.fori_loop(1, count, one, 0)

    tell(barrier, "pair", p, PAIRS)
    tell(barrier, "virt", v, VIRTS)

    for h in range(2):
        pltpu.make_async_copy(op[h], op[h], load_sem.at[h]).wait()
        def pack(s, carry, h=h):
            block = op[h][column_ref[(v * 2 + h) * SLOTS + s]]
            got[0][0][h][s] = block.reshape(4, 4, 8, BLOCK)
            return carry

        lax.fori_loop(0, SLOTS, pack, 0)

    pl.semaphore_wait(barrier, PAIRS + VIRTS - 2)
    tell(ready, "virt", v, VIRTS)
    pl.semaphore_wait(ready, VIRTS - 1)

    def place(xx, yy, zz, cc):
        return {"pair": (z_lo * 4 + xx) * 4 + yy, "virt": zz * 2 + cc}

    def remote(number, source, target, device):
        return pltpu.make_async_remote_copy(
            src_ref=source, dst_ref=target, send_sem=gather_out.at[number], recv_sem=gather_in.at[number],
            device_id=device, device_id_type=MESH,
        )

    everything = []

    def go(copy):
        copy.start()
        everything.append(copy)
        return copy

    def turn4(value, by):
        return lax.rem(value + (by + 4), 4)

    units = [(j, h) for j in JS for h in range(2)]
    base = {u: i * KINDS for i, u in enumerate(units)}
    core_copy = {}
    for h in range(2):
        mine = got[0][0][h]
        for j in JS:
            go(remote(base[j, h], mine.at[:, x, y], got[j][0][h].at[:, x, y], place(x, y, turn4(z_hi, j), core)))
    for h in range(2):
        core_copy[0, h] = go(
            remote(6 * KINDS + h, got[0][0][h], got[0][1][h], place(x, y, z_hi, 1 - core))
        )

    def along(h, by, first):
        if (h == 0) == first:
            return place(turn4(x, by), y, z_hi, core)
        return place(x, turn4(y, by), z_hi, core)

    def view(unit, a, b, slots=slice(None)):
        j, h = unit
        i, k = (a, b) if h == 0 else (b, a)
        return got[j][0][h].at[slots, i, k]

    low, high = pl.ds(0, SLOTS // 2), pl.ds(SLOTS // 2, SLOTS // 2)
    whole = slice(None)

    def own(h):
        return (x, y) if h == 0 else (y, x)

    def from_z(unit):
        number = base[unit]
        a, b = own(unit[1])
        remote(number, view(unit, a, b), view(unit, a, b), place(x, y, z_hi, core)).wait_recv()
        for kind, by in ((1, 1), (2, -1)):
            go(remote(number + kind, view(unit, a, b), view(unit, a, b), along(unit[1], by, True)))

    def first_forward(unit):
        number = base[unit]
        a, b = own(unit[1])
        for kind, by, part in ((1, 1, low), (2, -1, high)):
            behind = turn4(a, -by)
            block = view(unit, behind, b)
            remote(number + kind, block, block, along(unit[1], by, True)).wait_recv()
            block = view(unit, behind, b, part)
            go(remote(number + kind + 2, block, block, along(unit[1], by, True)))

    def second(unit):
        number = base[unit]
        a, b = own(unit[1])
        for kind, by, part in ((3, 1, low), (4, -1, high)):
            block = view(unit, turn4(a, 2), b, part)
            remote(number + kind, block, block, along(unit[1], by, True)).wait_recv()
        for kind, by in ((5, 1), (6, -1)):
            block = view(unit, whole, b)
            go(remote(number + kind, block, block, along(unit[1], by, False)))

    def second_forward(unit):
        number = base[unit]
        a, b = own(unit[1])
        for kind, by, part in ((5, 1, low), (6, -1, high)):
            behind = turn4(b, -by)
            block = view(unit, whole, behind)
            remote(number + kind, block, block, along(unit[1], by, False)).wait_recv()
            block = view(unit, whole, behind, part)
            go(remote(number + kind + 2, block, block, along(unit[1], by, False)))

    def complete(unit):
        number = base[unit]
        a, b = own(unit[1])
        for kind, by, part in ((7, 1, low), (8, -1, high)):
            block = view(unit, whole, turn4(b, 2), part)
            remote(number + kind, block, block, along(unit[1], by, False)).wait_recv()
        j, h = unit
        core_copy[unit] = go(
            remote(number + 9, got[j][0][h], got[j][1][h], place(x, y, z_hi, 1 - core))
        )

    def row_of(j, cc):
        return turn4(z_hi, -j) * 2 + (core if cc == 0 else 1 - core)

    def split_amplitudes():
        def one(i, carry):
            j = lax.rem(turn4(z_hi, 0) - i // 2 + 4, 4)
            k = j * 2 + lax.rem(i + core, 2)
            for h in range(2):
                value = amp[:, pl.ds(pl.multiple_of(i * ROWS + h * BLOCK, BLOCK), BLOCK)]
                a, b = split(value)
                lanes = pl.ds(pl.multiple_of(k * ROWS + h * BLOCK, BLOCK), BLOCK)
                a_high[:, lanes] = a
                a_low[:, lanes] = b
            return carry

        lax.fori_loop(0, VIRTS, one, 0)

    def expand(j, cc, h):
        k = j * 2 + cc
        source = got[j][cc][h]
        first = (row_of(j, cc) * 2 + h) * BLOCKS
        rows = pl.ds(k * ROWS + h * BLOCK, BLOCK)

        def one(c, carry):
            block = source[slot_ref[first + c]].reshape(BLOCK, BLOCK) * flag_ref[first + c]
            a, b = split(block)
            lanes = pl.ds(pl.multiple_of(c * BLOCK, BLOCK), BLOCK)
            w_high[rows, lanes] = a
            w_low[rows, lanes] = b
            return carry

        lax.fori_loop(0, BLOCKS, one, 0)

    def partial(k):
        rows = pl.ds(k * ROWS, ROWS)

        def one(n, carry):
            lanes = pl.ds(pl.multiple_of(n * 512, 512), 512)
            value = three_dots(a_high[:, rows], a_low[:, rows], w_high[rows, lanes], w_low[rows, lanes])
            if k == 0:
                prod[:, lanes] = value
            else:
                prod[:, lanes] += value
            return carry

        lax.fori_loop(0, WIDTH // 512, one, 0)

    def full():
        def one(n, carry):
            lanes = pl.ds(pl.multiple_of(n * 256, 256), 256)
            prod[:, lanes] = three_dots(a_high[...], a_low[...], w_high[:, lanes], w_low[:, lanes])
            return carry

        lax.fori_loop(0, WIDTH // 256, one, 0)

    def scatter(sweep, h):
        lanes = pl.ds(pl.multiple_of(v * BLOCK, BLOCK), BLOCK)

        def flip(w):
            block = prod[h * BLOCK:(h + 1) * BLOCK, pl.ds(pl.multiple_of(w * ROWS, ROWS), ROWS)]
            turned_in[h][w] = block.T.reshape(PAIRS, SLAB, BLOCK)

        def send(w):
            def one(step, carry):
                pair = lax.rem(p + step, PAIRS)
                pltpu.make_async_remote_copy(
                    src_ref=turned_in[h].at[w, pair], dst_ref=spread[sweep][h].at[p, :, lanes],
                    send_sem=hop_out.at[sweep * 4 + h], recv_sem=hop_in.at[sweep * 4 + h],
                    device_id={"pair": pair, "virt": w}, device_id_type=MESH,
                ).start()
                return carry

            return one

        def others(i, carry):
            w = lax.rem(v + i, VIRTS)
            flip(w)
            lax.fori_loop(0, PAIRS, send(w), 0)
            return carry

        lax.fori_loop(1, VIRTS, others, 0)
        flip(v)
        lax.fori_loop(1, PAIRS, send(v), 0)
        pltpu.make_async_copy(
            turned_in[h].at[v, p], spread[sweep][h].at[p, :, lanes], hop_in.at[sweep * 4 + h]
        ).start()

    def give(sweep, h):
        number = sweep * 4 + h
        pltpu.make_async_copy(spread[sweep][h], spread[sweep][h], hop_in.at[number]).wait()
        number += 2

        def one(step, carry):
            pair = lax.rem(p + step, PAIRS)
            turned[h][pair] = spread[sweep][h][partner_ref[pair]]
            pltpu.make_async_remote_copy(
                src_ref=turned[h].at[pair], dst_ref=mirror[sweep][h].at[p],
                send_sem=hop_out.at[number], recv_sem=hop_in.at[number],
                device_id={"pair": pair}, device_id_type=MESH,
            ).start()
            return carry

        lax.fori_loop(1, PAIRS, one, 0)
        turned[h][p] = spread[sweep][h][partner_ref[p]]
        pltpu.make_async_copy(turned[h].at[p], mirror[sweep][h].at[p], hop_in.at[number]).start()

    def combine(sweep, h):
        number = sweep * 4 + 2 + h
        pltpu.make_async_copy(mirror[sweep][h], mirror[sweep][h], hop_in.at[number]).wait()
        side = own_ref[...]

        def one(i, carry):
            lanes = pl.ds(pl.multiple_of(i * ROWS + h * BLOCK, BLOCK), BLOCK)
            other = mirror[sweep][h][:, :, pl.ds(pl.multiple_of(i * BLOCK, BLOCK), BLOCK)]
            below = side + virt_ref[:1, lanes] + pair_ref[0]
            value = (ints[:, lanes] + prod[:, lanes] + other.reshape(ROWS, BLOCK)) / below
            if sweep == ITERS - 1:
                out_ref[:, lanes] = value
            else:
                j = lax.rem(z_hi - i // 2 + 4, 4)
                k = j * 2 + lax.rem(i + core, 2)
                a, b = split(value)
                lanes = pl.ds(pl.multiple_of(k * ROWS + h * BLOCK, BLOCK), BLOCK)
                a_high[:, lanes] = a
                a_low[:, lanes] = b
            return carry

        lax.fori_loop(0, VIRTS, one, 0)

    def drain(sweep):
        for h in range(HALVES):
            sent = turned_in[h].at[pl.ds(0, VIRTS - 1)]
            pltpu.make_async_copy(sent, sent, hop_out.at[sweep * 4 + h]).wait()
            sent = turned_in[h].at[0, pl.ds(0, PAIRS - 1)]
            pltpu.make_async_copy(sent, sent, hop_out.at[sweep * 4 + h]).wait()
            sent = turned[h].at[pl.ds(0, PAIRS - 1)]
            pltpu.make_async_copy(sent, sent, hop_out.at[sweep * 4 + 2 + h]).wait()

    for unit in units:
        from_z(unit)
    for unit in units:
        first_forward(unit)
    for unit in units:
        second(unit)
    loads[-2].wait()
    split_amplitudes()
    for h in range(2):
        expand(0, 0, h)
    partial(0)
    for unit in units:
        second_forward(unit)
    for h in range(2):
        core_copy[0, h].wait_recv()
        expand(0, 1, h)
    partial(1)
    for j in JS:
        for h in range(2):
            complete((j, h))
            expand(j, 0, h)
        partial(j * 2)
    for j in JS:
        for h in range(2):
            core_copy[j, h].wait_recv()
            expand(j, 1, h)
        partial(j * 2 + 1)
    loads[-1].wait()
    for sweep in range(ITERS):
        if sweep:
            full()
        for h in range(HALVES):
            scatter(sweep, h)
        for h in range(HALVES):
            give(sweep, h)
        for h in range(HALVES):
            combine(sweep, h)
        drain(sweep)
    for copy in everything:
        copy.wait_send()


def per_device(amplitudes, integrals, operator, virt_energy, pair_energy, block_mask, partner):
    v = lax.axis_index("virt")
    own = lax.dynamic_slice_in_dim(virt_energy, v * ROWS, ROWS)
    own = jnp.broadcast_to(own[:, None], (ROWS, BLOCK))
    virt = jnp.broadcast_to(virt_energy[None, :], (8, WIDTH))
    number = jnp.arange(BLOCKS)
    ahead = (number[None, :] < number[:, None]).astype(jnp.int32)
    slot = jnp.sum(block_mask[:, None, :] * ahead[None], axis=2)
    slot = jnp.where(block_mask > 0, slot, 0)
    hit = (slot[:, None, :] == jnp.arange(SLOTS)[None, :, None]) & (block_mask[:, None, :] > 0)
    columns = jnp.sum(jnp.where(hit, number[None, None, :], 0), axis=2)
    smem = pl.BlockSpec(memory_space=pltpu.SMEM)
    vmem = pl.BlockSpec(memory_space=pltpu.VMEM)
    hbm = pl.BlockSpec(memory_space=pl.ANY)
    slab = (PAIRS, SLAB, WIDTH // HALVES)
    result = pl.pallas_call(
        kernel,
        out_shape=jax.ShapeDtypeStruct((ROWS, WIDTH), F32),
        in_specs=[smem] * 5 + [hbm] * 3 + [vmem] * 2,
        out_specs=vmem,
        scratch_shapes=[pltpu.VMEM((ROWS, WIDTH), F32)] * 2
        + [pltpu.VMEM((BLOCKS, BLOCK, BLOCK), F32)] * 2
        + [pltpu.VMEM((ROWS, WIDTH), F32)]
        + [pltpu.VMEM((ROWS, WIDTH), BF16)] * 2
        + [pltpu.VMEM((WIDTH, WIDTH), BF16)] * 2
        + [pltpu.VMEM((SLOTS, 4, 4, 8, BLOCK), F32)] * 16
        + [pltpu.VMEM((VIRTS, PAIRS, SLAB, BLOCK), F32)] * 2
        + [pltpu.VMEM(slab, F32)] * 10
        + [
            pltpu.SemaphoreType.DMA((4,)),
            pltpu.SemaphoreType.DMA((6 * KINDS + 2,)),
            pltpu.SemaphoreType.DMA((6 * KINDS + 2,)),
            pltpu.SemaphoreType.DMA((8,)),
            pltpu.SemaphoreType.DMA((8,)),
            pltpu.SemaphoreType.REGULAR,
        ],
        compiler_params=pltpu.CompilerParams(
            collective_id=0, has_side_effects=True, vmem_limit_bytes=58 << 20
        ),
    )(
        partner, slot.reshape(-1), block_mask.astype(F32).reshape(-1), columns.reshape(-1), pair_energy,
        amplitudes[0], integrals[0], operator, own, virt,
    )
    return result[None]


def solution(mesh):
    return jax.shard_map(
        per_device,
        mesh=mesh,
        in_specs=(
            P("pair", "virt", None),
            P("pair", "virt", None),
            P("virt", None),
            P(),
            P("pair"),
            P(),
            P(),
        ),
        out_specs=P("pair", "virt", None),
        check_vma=False,
    )
```

time: 546 us -> 219 us (0.40)
  waiting for transfers between devices: 210 us -> 0 us
  Pallas kernels: 0 us -> 208 us
  blocking collectives: 174 us -> 0 us
  matrix products: 73.9 us -> 0 us
  local copies, waits for them, and re-layouts: 46.2 us -> 8.03 us
  starting transfers between devices: 16.2 us -> 0 us
  between operations: 14.2 us -> 0.67 us
  other arithmetic: 8.15 us -> 2.07 us
    pallas_call x0 -> x1, Pallas kernels: none -> 208 us  [per_device(): pl.pallas_call(kernel, out_shape=jax.ShapeDtypeStruct((ROWS, WIDTH), F32)...]
    all_to_all x4 -> x0, blocking collectives: 174 us -> none  [the longest x2 110 us: reflect(): lax.all_to_all(product, 'virt', split_axis=2, concat_axis=1, tiled=True)]
    all_gather x1 -> x0, waiting for transfers between devices: 162 us -> none  [per_device(): gathered = lax.all_gather(operator, 'virt', axis=0, tiled=True)]
    dot_general x2 -> x0, matrix products: 73.9 us -> none  [per_device(): jnp.einsum('prc,cb->prb', current, masked, precision=lax.Precision.HIGHEST)]
    all_to_all x2 -> x0, waiting for transfers between devices: 47.5 us -> none  [the longest x1 25.4 us: reverse_pairs(): lax.all_to_all(slabs, 'pair', split_axis=1, concat_axis=0, tiled=True)]
    all_to_all x2 -> x0, starting transfers between devices: 16.2 us -> none  [the longest x1 8.28 us: reverse_pairs(): lax.all_to_all(slabs, 'pair', split_axis=1, concat_axis=0, tiled=True)]
    dot_general x2 -> x0, local copies, waits for them, and re-layouts: 12.3 us -> none  [per_device(): jnp.einsum('prc,cb->prb', current, masked, precision=lax.Precision.HIGHEST)]
    mul x1 -> x0, local copies, waits for them, and re-layouts: 6.87 us -> none  [per_device(): gathered.reshape(block_count, block_size, block_count, block_size)]
  transfers between devices with their start and end apart: 3 -> 0, of which waited for: 3 -> 0; matrix products, arithmetic and copies ran while one was open for 1% -> 0% of each run, Pallas kernels for 0% -> 0%
where the time goes in v2:
time: 219 us; the launch traced here: 218 us
  Pallas kernels  208 us (95%)
  local copies, waits for them, and re-layouts  8.03 us (4%)
    pallas_call x1, Pallas kernels, per_device(): pl.pallas_call(kernel, out_shape=jax.ShapeDtypeStruct((ROWS, WIDTH), F32)...  208 us

profile of v2, /device:TPU:30, one launch (start us, length us, event | category | flops | bytes accessed | tf_op | source)
XLA Modules:
  0.0 218.3 jit_solution(3179422464115232502)
XLA Ops:
  0.7 0.8 dynamic_slice.3
  1.4 1.0 multiply_reduce_fusion
  2.5 0.8 broadcast_select_fusion
  3.2 0.6 reshape.29.flag_ref
  3.9 0.6 reshape.28.slot_ref
  4.5 0.2 select_reduce_fusion
  4.8 0.1 copy.8
  4.9 0.7 reshape.30.column_ref
  5.6 1.3 broadcast_in_dim.19.virt_ref
  6.9 0.8 broadcast_in_dim.18.own_ref
  7.6 207.5 %shard_map.73 = f32[256,2048]{1,0:T(8,128)} custom-call(s32[32]{0:T(128)} %partner_ref.1, s32[256]{0:T(256)} %reshape.28.slot_ref, f32[256]{0:T(256)} %reshape.29.flag_ref, s32[160]{0:T(256)} %reshape.30.column_ref, f32[1]{0:T(128)S(6)} %copy.10.pair_ref, f32[256,2048]{1,0:T(8,128)} %bitcast.4, f32[256,2048]{1,0:T(8,128)} %bitcast.5, f32[256,2048]{1,0:T(8,128)} %op_hbm.1, ...), custom_call_target="tpu_custom_call" | custom-call | tf_op jit(solution)/shard_map/pallas_call | solution.py:377
  215.2 3.1 %copy.11 = f32[1,256,2048]{2,1,0:T(8,128)} copy(f32[1,256,2048]{2,1,0:T(8,128)} %bitcast.3) | data formatting | bytes 4194304
  (1 shorter events, 0.0 us)

commit v3 on v2

v3 whole, which is shorter than its diff:
```python
import jax
import jax.numpy as jnp
from jax import lax
from jax.experimental import pallas as pl
from jax.experimental.pallas import tpu as pltpu
from jax.sharding import PartitionSpec as P

ITERS = 2
MESH = pl.DeviceIdType.MESH
PAIRS, VIRTS = 32, 8
TOTAL = PAIRS * VIRTS
WIDTH, ROWS, BLOCK, BLOCKS, SLOTS = 2048, 256, 128, 16, 10
SLAB = 16
PLANE = PAIRS // 2
F32, BF16 = jnp.float32, jnp.bfloat16
JS = (1, 3, 2)
KINDS = 13
PIECES = {
    (0, 0): (0, 0), (0, 1): (0, 1), (1, 0): (1, 0), (3, 0): (1, 1),
    (1, 1): (2, 0), (3, 1): (2, 1), (2, 0): (3, 0), (2, 1): (3, 1),
}
CHUNKS = 4
ORDER = {piece: c * 2 + plane for piece, (c, plane) in PIECES.items()}


def split(value):
    high = value.astype(BF16)
    return high, (value - high.astype(F32)).astype(BF16)


def three_dots(a_high, a_low, b_high, b_low):
    def dot(a, b):
        return jnp.dot(a, b, preferred_element_type=F32)

    return dot(a_high, b_high) + (dot(a_high, b_low) + dot(a_low, b_high))


def kernel(
    partner_ref, mask_ref, pair_ref, amp_hbm, int_hbm, op_hbm, virt_ref,
    out_ref,
    amp, ints, op0, op1, side, prod0, prod1, a_high, a_low, w_high, w_low, *rest,
):
    got = [[[rest[(j * 2 + cc) * 2 + h] for h in range(2)] for cc in range(2)] for j in range(4)]
    rest = rest[16:]
    turned_in, spread, turned, mirror = (
        rest[0:4], (rest[4:8], rest[8:12]), rest[12:16], (rest[16:20], rest[20:24])
    )
    load_sem, gather_out, gather_in, hop_out, hop_in, ready = rest[24:]

    p, v = lax.axis_index("pair"), lax.axis_index("virt")
    z_lo, x, y = p // 16, lax.rem(p // 4, 4), lax.rem(p, 4)
    z_hi, core = v // 2, lax.rem(v, 2)
    op, prods = (op0, op1), (prod0, prod1)
    barrier = pltpu.get_barrier_semaphore()

    loads = [
        pltpu.make_async_copy(
            op_hbm.at[pl.ds(h * BLOCK, BLOCK), pl.ds(c * BLOCK, BLOCK)], op[h].at[c], load_sem.at[h]
        )
        for h in range(2) for c in range(BLOCKS)
    ] + [
        pltpu.make_async_copy(amp_hbm, amp, load_sem.at[2]),
        pltpu.make_async_copy(int_hbm, ints, load_sem.at[3]),
    ]
    for load in loads:
        load.start()

    def tell(semaphore, axis, mine, count):
        def one(step, carry):
            pl.semaphore_signal(
                semaphore, inc=1, device_id={axis: lax.rem(mine + step, count)}, device_id_type=MESH
            )
            return carry

        lax.fori_loop(1, count, one, 0)

    tell(barrier, "pair", p, PAIRS)
    tell(barrier, "virt", v, VIRTS)

    for h in range(2):
        pltpu.make_async_copy(op[h], op[h], load_sem.at[h]).wait()
        def find(c, carry, h=h):
            count, columns = carry
            here = mask_ref[v * 2 + h, c]
            columns = tuple(
                jnp.where((count == s) & (here > 0), c, column) for s, column in enumerate(columns)
            )
            return count + here, columns

        zero = jnp.int32(0)
        _, columns = lax.fori_loop(0, BLOCKS, find, (zero, (zero,) * SLOTS))
        for s in range(SLOTS):
            got[0][0][h][s] = op[h][columns[s]].reshape(4, 4, 8, BLOCK)

    pl.semaphore_wait(barrier, PAIRS + VIRTS - 2)
    tell(ready, "virt", v, VIRTS)
    pl.semaphore_wait(ready, VIRTS - 1)

    def place(xx, yy, zz, cc):
        return {"pair": (z_lo * 4 + xx) * 4 + yy, "virt": zz * 2 + cc}

    def remote(number, source, target, device):
        return pltpu.make_async_remote_copy(
            src_ref=source, dst_ref=target, send_sem=gather_out.at[number], recv_sem=gather_in.at[number],
            device_id=device, device_id_type=MESH,
        )

    everything = []

    def go(copy):
        copy.start()
        everything.append(copy)
        return copy

    def turn4(value, by):
        return lax.rem(value + (by + 4), 4)

    units = [(j, h) for j in JS for h in range(2)]
    base = {u: i * KINDS for i, u in enumerate(units)}
    core_copy = {}
    for h in range(2):
        mine = got[0][0][h]
        for j in JS:
            go(remote(base[j, h], mine.at[:, x, y], got[j][0][h].at[:, x, y], place(x, y, turn4(z_hi, j), core)))
    for h in range(2):
        core_copy[0, h] = go(
            remote(6 * KINDS + h, got[0][0][h], got[0][1][h], place(x, y, z_hi, 1 - core))
        )

    def along(h, by, first):
        if (h == 0) == first:
            return place(turn4(x, by), y, z_hi, core)
        return place(x, turn4(y, by), z_hi, core)

    def view(unit, a, b, slots=slice(None)):
        j, h = unit
        i, k = (a, b) if h == 0 else (b, a)
        return got[j][0][h].at[slots, i, k]

    low, high = pl.ds(0, SLOTS // 2), pl.ds(SLOTS // 2, SLOTS // 2)
    whole = slice(None)

    def own(h):
        return (x, y) if h == 0 else (y, x)

    def from_z(unit):
        number = base[unit]
        a, b = own(unit[1])
        remote(number, view(unit, a, b), view(unit, a, b), place(x, y, z_hi, core)).wait_recv()
        for kind, by in ((1, 1), (2, -1)):
            go(remote(number + kind, view(unit, a, b), view(unit, a, b), along(unit[1], by, True)))

    def first_forward(unit):
        number = base[unit]
        a, b = own(unit[1])
        for kind, by, part in ((1, 1, low), (2, -1, high)):
            behind = turn4(a, -by)
            block = view(unit, behind, b)
            remote(number + kind, block, block, along(unit[1], by, True)).wait_recv()
            block = view(unit, behind, b, part)
            go(remote(number + kind + 2, block, block, along(unit[1], by, True)))

    def second(unit):
        number = base[unit]
        a, b = own(unit[1])
        for kind, by, part in ((3, 1, low), (4, -1, high)):
            block = view(unit, turn4(a, 2), b, part)
            remote(number + kind, block, block, along(unit[1], by, True)).wait_recv()
        for kind, by in ((5, 1), (6, -1)):
            block = view(unit, whole, b)
            go(remote(number + kind, block, block, along(unit[1], by, False)))
        to_core(unit, 0, b)

    def second_forward(unit):
        number = base[unit]
        a, b = own(unit[1])
        for kind, by, part in ((5, 1, low), (6, -1, high)):
            behind = turn4(b, -by)
            block = view(unit, whole, behind)
            remote(number + kind, block, block, along(unit[1], by, False)).wait_recv()
            block = view(unit, whole, behind, part)
            go(remote(number + kind + 2, block, block, along(unit[1], by, False)))
        to_core(unit, 1, turn4(b, 1))
        to_core(unit, 2, turn4(b, -1))

    def complete(unit):
        number = base[unit]
        a, b = own(unit[1])
        for kind, by, part in ((7, 1, low), (8, -1, high)):
            block = view(unit, whole, turn4(b, 2), part)
            remote(number + kind, block, block, along(unit[1], by, False)).wait_recv()
        to_core(unit, 3, turn4(b, 2))

    def to_core(unit, part, b):
        j, h = unit
        where = (slice(None), slice(None), b) if h == 0 else (slice(None), b)
        core_copy[unit, part] = go(
            remote(
                base[unit] + 9 + part, got[j][0][h].at[where], got[j][1][h].at[where],
                place(x, y, z_hi, 1 - core),
            )
        )

    def from_core(unit):
        for part in range(4):
            core_copy[unit, part].wait_recv()

    def row_of(j, cc):
        return turn4(z_hi, -j) * 2 + (core if cc == 0 else 1 - core)

    def columns_of(j, core_of, h):
        start = (turn4(z_hi, -j) * 2 + core_of) * ROWS + h * BLOCK
        return pl.ds(pl.multiple_of(start, BLOCK), BLOCK)

    def depth_of(j, core_of, h):
        start = (ORDER[j, h] * 2 + lax.rem(core_of + core, 2)) * BLOCK
        return pl.ds(pl.multiple_of(start, BLOCK), BLOCK)

    def split_amplitudes():
        for j, h in PIECES:
            def one(core_of, carry, j=j, h=h):
                lanes = depth_of(j, core_of, h)
                a_high[:, lanes], a_low[:, lanes] = split(amp[:, columns_of(j, core_of, h)])
                return carry

            lax.fori_loop(0, 2, one, 0)

    def expand(j, cc, h):
        source = got[j][cc][h]
        row = row_of(j, cc) * 2 + h
        rows = pl.ds((ORDER[j, h] * 2 + cc) * BLOCK, BLOCK)

        def one(c, count):
            here = mask_ref[row, c]
            slot = jnp.minimum(count, SLOTS - 1)
            block = source[slot].reshape(BLOCK, BLOCK) * here.astype(F32)
            lanes = pl.ds(pl.multiple_of(c * BLOCK, BLOCK), BLOCK)
            w_high[rows, lanes], w_low[rows, lanes] = split(block)
            return count + here

        lax.fori_loop(0, BLOCKS, one, jnp.int32(0))

    def multiply(prod, first, count, n, add):
        rows = pl.ds(first * ROWS, count * ROWS)
        lanes = pl.ds(pl.multiple_of(n * 512, 512), 512)
        value = three_dots(a_high[:, rows], a_low[:, rows], w_high[rows, lanes], w_low[rows, lanes])
        if add:
            prod[:, lanes] += value
        else:
            prod[:, lanes] = value

    def multiply_all(prod, first, count, add):
        def one(n, carry):
            multiply(prod, first, count, n, add)
            return carry

        lax.fori_loop(0, WIDTH // 512, one, 0)

    xy = x * 4 + y

    def landing(sweep, c):
        return spread[sweep][c].at[p, :, pl.ds(pl.multiple_of(core * BLOCK, BLOCK), BLOCK)]

    def flip(sweep, c):
        for (j, h), (chunk, plane) in PIECES.items():
            if chunk != c:
                continue

            def one(other, carry, j=j, h=h, plane=plane):
                w = turn4(z_hi, j) * 2 + lax.rem(core + other, 2)
                lanes = pl.ds(pl.multiple_of(w * ROWS, ROWS), ROWS)
                block = prods[sweep][h * BLOCK:(h + 1) * BLOCK, lanes]
                turned_in[c][plane * 2 + other] = block.T.reshape(PLANE, SLAB, BLOCK)
                return carry

            lax.fori_loop(0, 2, one, 0)

    def send(sweep, c, other, step):
        number = sweep * 8 + c
        i = lax.rem(xy + step, PLANE)
        for (j, h), (chunk, plane) in PIECES.items():
            if chunk != c:
                continue
            w = turn4(z_hi, j) * 2 + lax.rem(core + other, 2)
            pltpu.make_async_remote_copy(
                src_ref=turned_in[c].at[plane * 2 + other, i], dst_ref=landing(sweep, c),
                send_sem=hop_out.at[number], recv_sem=hop_in.at[number],
                device_id={"pair": plane * PLANE + i, "virt": w}, device_id_type=MESH,
            ).start()

    def scatter(sweep, c):
        def one(step, carry):
            send(sweep, c, step // PLANE, lax.rem(step, PLANE))
            return carry

        if c:
            lax.fori_loop(0, PAIRS, one, 0)
            return
        lax.fori_loop(1, PAIRS, one, 0)
        pltpu.make_async_copy(
            turned_in[c].at[z_lo * 2, xy], landing(sweep, c), hop_in.at[sweep * 8]
        ).start()
        pltpu.make_async_remote_copy(
            src_ref=turned_in[c].at[2 - z_lo * 2, xy], dst_ref=landing(sweep, c),
            send_sem=hop_out.at[sweep * 8], recv_sem=hop_in.at[sweep * 8],
            device_id={"pair": (1 - z_lo) * PLANE + xy, "virt": v}, device_id_type=MESH,
        ).start()

    def give(sweep, c, beside=None):
        number = sweep * 8 + c
        pltpu.make_async_copy(spread[sweep][c], spread[sweep][c], hop_in.at[number]).wait()
        number += 4

        def one(step, carry):
            pair = lax.rem(p + lax.rem(step * 13, PAIRS), PAIRS)
            turned[c][pair] = spread[sweep][c][partner_ref[pair]]
            pltpu.make_async_remote_copy(
                src_ref=turned[c].at[pair], dst_ref=mirror[sweep][c].at[p],
                send_sem=hop_out.at[number], recv_sem=hop_in.at[number],
                device_id={"pair": pair}, device_id_type=MESH,
            ).start()
            if beside is not None:
                send(sweep, beside, step // PLANE, lax.rem(step, PLANE))
            return carry

        lax.fori_loop(1, PAIRS, one, 0)
        if beside is not None:
            send(sweep, beside, 0, 0)
        turned[c][p] = spread[sweep][c][partner_ref[p]]
        pltpu.make_async_copy(turned[c].at[p], mirror[sweep][c].at[p], hop_in.at[number]).start()

    def exchange(sweep, first, count):
        multiply(prods[sweep], first, count, z_hi, True)
        flip(sweep, 0)
        scatter(sweep, 0)
        for j in (1, 3):
            multiply(prods[sweep], first, count, turn4(z_hi, j), True)
        flip(sweep, 1)
        scatter(sweep, 1)
        flip(sweep, 2)
        multiply(prods[sweep], first, count, turn4(z_hi, 2), True)
        give(sweep, 0, 2)
        flip(sweep, 3)
        give(sweep, 1, 3)
        give(sweep, 2)
        give(sweep, 3)

    def combine(sweep, chunk):
        number = sweep * 8 + 4 + chunk
        pltpu.make_async_copy(mirror[sweep][chunk], mirror[sweep][chunk], hop_in.at[number]).wait()
        for (j, h), (c, plane) in PIECES.items():
            if c != chunk:
                continue

            def one(core_of, carry, j=j, h=h, plane=plane):
                lanes = columns_of(j, core_of, h)
                place = pl.ds(pl.multiple_of(core_of * BLOCK, BLOCK), BLOCK)
                other = mirror[sweep][chunk][plane * PLANE:(plane + 1) * PLANE, :, place]
                below = side[...] + virt_ref[:, lanes] + pair_ref[0]
                value = (ints[:, lanes] + prods[sweep][:, lanes] + other.reshape(ROWS, BLOCK)) / below
                if sweep == ITERS - 1:
                    out_ref[:, lanes] = value
                else:
                    depth = depth_of(j, core_of, h)
                    a_high[:, depth], a_low[:, depth] = split(value)
                return carry

            lax.fori_loop(0, 2, one, 0)

    def drain(sweep):
        sent = turned_in[0].at[pl.ds(0, 3)]
        pltpu.make_async_copy(sent, sent, hop_out.at[sweep * 8]).wait()
        sent = turned_in[0].at[0, pl.ds(0, PLANE - 1)]
        pltpu.make_async_copy(sent, sent, hop_out.at[sweep * 8]).wait()
        for c in range(CHUNKS):
            if c:
                pltpu.make_async_copy(turned_in[c], turned_in[c], hop_out.at[sweep * 8 + c]).wait()
            sent = turned[c].at[pl.ds(0, PAIRS - 1)]
            pltpu.make_async_copy(sent, sent, hop_out.at[sweep * 8 + 4 + c]).wait()

    near, far = units[:4], units[4:]
    for group in (near, far):
        for step in (from_z, first_forward, second):
            for unit in group:
                step(unit)
    own_energy = virt_ref[:, pl.ds(pl.multiple_of(v * ROWS, ROWS), ROWS)]
    side[...] = jnp.broadcast_to(own_energy, (BLOCK, ROWS)).T
    loads[-2].wait()
    split_amplitudes()
    for h in range(2):
        expand(0, 0, h)
    for unit in near:
        second_forward(unit)
    for h in range(2):
        core_copy[0, h].wait_recv()
        expand(0, 1, h)
    multiply_all(prods[0], 0, 2, False)
    for unit in far:
        second_forward(unit)
    for unit in units:
        complete(unit)
        expand(unit[0], 0, unit[1])
    for unit in units:
        from_core(unit)
        expand(unit[0], 1, unit[1])
        if unit != units[-1]:
            multiply_all(prods[0], ORDER[unit], 1, True)
    loads[-1].wait()
    exchange(0, ORDER[units[-1]], 1)
    combine(0, 0)
    combine(0, 1)
    multiply_all(prods[1], 0, 4, False)
    combine(0, 2)
    multiply_all(prods[1], 4, 2, True)
    combine(0, 3)
    drain(0)
    exchange(1, 6, 2)
    for c in range(CHUNKS):
        combine(1, c)
    drain(1)
    for copy in everything:
        copy.wait_send()


def per_device(amplitudes, integrals, operator, virt_energy, pair_energy, block_mask, partner):
    smem = pl.BlockSpec(memory_space=pltpu.SMEM)
    vmem = pl.BlockSpec(memory_space=pltpu.VMEM)
    hbm = pl.BlockSpec(memory_space=pl.ANY)
    slab = (PAIRS, SLAB, 2 * BLOCK)
    result = pl.pallas_call(
        kernel,
        out_shape=jax.ShapeDtypeStruct((ROWS, WIDTH), F32),
        in_specs=[smem] * 3 + [hbm] * 3 + [vmem],
        out_specs=vmem,
        scratch_shapes=[pltpu.VMEM((ROWS, WIDTH), F32)] * 2
        + [pltpu.VMEM((BLOCKS, BLOCK, BLOCK), F32)] * 2
        + [pltpu.VMEM((ROWS, BLOCK), F32)]
        + [pltpu.VMEM((ROWS, WIDTH), F32)] * 2
        + [pltpu.VMEM((ROWS, WIDTH), BF16)] * 2
        + [pltpu.VMEM((WIDTH, WIDTH), BF16)] * 2
        + [pltpu.VMEM((SLOTS, 4, 4, 8, BLOCK), F32)] * 16
        + [pltpu.VMEM((4, PLANE, SLAB, BLOCK), F32)] * 4
        + [pltpu.VMEM(slab, F32)] * 20
        + [
            pltpu.SemaphoreType.DMA((4,)),
            pltpu.SemaphoreType.DMA((6 * KINDS + 2,)),
            pltpu.SemaphoreType.DMA((6 * KINDS + 2,)),
            pltpu.SemaphoreType.DMA((16,)),
            pltpu.SemaphoreType.DMA((16,)),
            pltpu.SemaphoreType.REGULAR,
        ],
        compiler_params=pltpu.CompilerParams(
            collective_id=0, has_side_effects=True, vmem_limit_bytes=58 << 20
        ),
    )(
        partner, block_mask, pair_energy, amplitudes[0], integrals[0], operator, virt_energy[None],
    )
    return result[None]


def solution(mesh):
    return jax.shard_map(
        per_device,
        mesh=mesh,
        in_specs=(
            P("pair", "virt", None),
            P("pair", "virt", None),
            P("virt", None),
            P(),
            P("pair"),
            P(),
            P(),
        ),
        out_specs=P("pair", "virt", None),
        check_vma=False,
    )
```

time: 219 us -> 195 us (0.89)
  the two profiles are of different devices: /device:TPU:30 before, /device:TPU:32 now
where the time goes in v3:
time: 195 us
  Pallas kernels  191 us (98%)
  local copies, waits for them, and re-layouts  3.14 us (2%)
    pallas_call x1, Pallas kernels, per_device(): pl.pallas_call(kernel, out_shape=jax.ShapeDtypeStruct((ROWS, WIDTH), F32)...  191 us

profile of v3, /device:TPU:32, one launch (start us, length us, event | category | flops | bytes accessed | tf_op | source)
XLA Modules:
  0.0 194.6 jit_solution(1709248091809247719)
XLA Ops:
  0.7 190.8 %shard_map.73 = f32[256,2048]{1,0:T(8,128)} custom-call(s32[32]{0:T(128)} %partner_ref.1, s32[16,16]{1,0:T(8,128)} %mask_ref.1, f32[1]{0:T(128)S(6)} %copy.9.pair_ref, f32[256,2048]{1,0:T(8,128)} %bitcast.5, f32[256,2048]{1,0:T(8,128)} %bitcast.6, f32[256,2048]{1,0:T(8,128)} %op_hbm.1, f32[1,2048]{1,0:T(1,128)} %bitcast.7), custom_call_target="tpu_custom_call" | custom-call | tf_op jit(solution)/shard_map/pallas_call | solution.py:430
  191.5 3.1 %copy.10 = f32[1,256,2048]{2,1,0:T(8,128)} copy(f32[1,256,2048]{2,1,0:T(8,128)} %bitcast.4) | data formatting | bytes 4194304

commit v4 on v3

--- a/solution.py
+++ b/solution.py
@@ -13,7 +13,8 @@
 SLAB = 16
 PLANE = PAIRS // 2
 F32, BF16 = jnp.float32, jnp.bfloat16
-JS = (1, 3, 2)
+NEAR, FAR, DIRECT = ((1, 1), (3, 0)), ((2, 0), (2, 1)), ((1, 0), (3, 1))
+PARTS = 5
 KINDS = 13
 PIECES = {
     (0, 0): (0, 0), (0, 1): (0, 1), (1, 0): (1, 0), (3, 0): (1, 1),
@@ -115,17 +116,53 @@
     def turn4(value, by):
         return lax.rem(value + (by + 4), 4)
 
-    units = [(j, h) for j in JS for h in range(2)]
+    units = NEAR + FAR + DIRECT
     base = {u: i * KINDS for i, u in enumerate(units)}
     core_copy = {}
-    for h in range(2):
-        mine = got[0][0][h]
-        for j in JS:
-            go(remote(base[j, h], mine.at[:, x, y], got[j][0][h].at[:, x, y], place(x, y, turn4(z_hi, j), core)))
+    for j, h in NEAR + FAR:
+        block = got[0][0][h].at[:, x, y]
+        go(remote(base[j, h], block, got[j][0][h].at[:, x, y], place(x, y, turn4(z_hi, j), core)))
     for h in range(2):
         core_copy[0, h] = go(
             remote(6 * KINDS + h, got[0][0][h], got[0][1][h], place(x, y, z_hi, 1 - core))
         )
+
+    def direct(unit, part, first):
+        j, h = unit
+        slots = pl.ds(part * (SLOTS // PARTS), SLOTS // PARTS)
+        z = turn4(z_hi, z_lo) if j == 1 else turn4(z_hi, z_lo - 1)
+        device = {"pair": ((1 - z_lo) * 4 + x) * 4 + y, "virt": z * 2 + core}
+        source = got[0 if first else j][0][h].at[slots]
+        return remote(base[unit] + part, source, got[j][0][h].at[slots], device)
+
+    def direct_start():
+        for unit in DIRECT:
+            @pl.when(z_lo == (1 if unit[0] == 1 else 0))
+            def _():
+                for part in range(PARTS):
+                    direct(unit, part, True).start()
+
+    def direct_pass(part):
+        for unit in DIRECT:
+            @pl.when(z_lo != (1 if unit[0] == 1 else 0))
+            def _():
+                direct(unit, part, False).wait_recv()
+                direct(unit, part, False).start()
+
+    def direct_end(unit):
+        j, h = unit
+        for part in range(PARTS):
+            @pl.when(z_lo == (1 if j == 1 else 0))
+            def _():
+                direct(unit, part, False).wait_recv()
+
+            slots = pl.ds(part * (SLOTS // PARTS), SLOTS // PARTS)
+            core_copy[unit, part] = go(
+                remote(
+                    base[unit] + PARTS + part, got[j][0][h].at[slots], got[j][1][h].at[slots],
+                    place(x, y, z_hi, 1 - core),
+                )
+            )
 
     def along(h, by, first):
         if (h == 0) == first:
@@ -202,7 +239,7 @@
         )
 
     def from_core(unit):
-        for part in range(4):
+        for part in range(PARTS if unit in DIRECT else 4):
             core_copy[unit, part].wait_recv()
 
     def row_of(j, cc):
@@ -378,35 +415,54 @@
             sent = turned[c].at[pl.ds(0, PAIRS - 1)]
             pltpu.make_async_copy(sent, sent, hop_out.at[sweep * 8 + 4 + c]).wait()
 
-    near, far = units[:4], units[4:]
-    for group in (near, far):
-        for step in (from_z, first_forward, second):
-            for unit in group:
-                step(unit)
+    for unit in NEAR + FAR:
+        from_z(unit)
+    direct_start()
+    for unit in NEAR + FAR:
+        first_forward(unit)
+    for unit in NEAR + FAR:
+        second(unit)
+    direct_pass(0)
+    direct_pass(1)
     own_energy = virt_ref[:, pl.ds(pl.multiple_of(v * ROWS, ROWS), ROWS)]
     side[...] = jnp.broadcast_to(own_energy, (BLOCK, ROWS)).T
     loads[-2].wait()
     split_amplitudes()
     for h in range(2):
         expand(0, 0, h)
-    for unit in near:
+    direct_pass(2)
+    for unit in NEAR:
         second_forward(unit)
     for h in range(2):
         core_copy[0, h].wait_recv()
         expand(0, 1, h)
+    direct_pass(3)
+    for unit in FAR:
+        second_forward(unit)
+    direct_pass(4)
     multiply_all(prods[0], 0, 2, False)
-    for unit in far:
-        second_forward(unit)
-    for unit in units:
+
+    def use(unit):
+        from_core(unit)
+        expand(unit[0], 1, unit[1])
+        if unit != FAR[1]:
+            multiply_all(prods[0], ORDER[unit], 1, True)
+
+    for unit in NEAR:
         complete(unit)
         expand(unit[0], 0, unit[1])
-    for unit in units:
-        from_core(unit)
-        expand(unit[0], 1, unit[1])
-        if unit != units[-1]:
-            multiply_all(prods[0], ORDER[unit], 1, True)
+    for unit in DIRECT:
+        direct_end(unit)
+        expand(unit[0], 0, unit[1])
+    for unit in NEAR:
+        use(unit)
+    for unit in FAR:
+        complete(unit)
+        expand(unit[0], 0, unit[1])
+    for unit in DIRECT + FAR:
+        use(unit)
     loads[-1].wait()
-    exchange(0, ORDER[units[-1]], 1)
+    exchange(0, ORDER[FAR[1]], 1)
     combine(0, 0)
     combine(0, 1)
     multiply_all(prods[1], 0, 4, False)
@@ -420,6 +476,9 @@
     drain(1)
     for copy in everything:
         copy.wait_send()
+    for unit in DIRECT:
+        for part in range(PARTS):
+            direct(unit, part, False).wait_send()
 
 
 def per_device(amplitudes, integrals, operator, virt_energy, pair_energy, block_mask, partner):

time: 195 us -> 187 us (0.959)
  the two profiles are of different devices: /device:TPU:32 before, /device:TPU:30 now
where the time goes in v4:
time: 187 us; the launch traced here: 183 us
  Pallas kernels  180 us (96%)
  local copies, waits for them, and re-layouts  3.14 us (2%)
    pallas_call x1, Pallas kernels, per_device(): pl.pallas_call(kernel, out_shape=jax.ShapeDtypeStruct((ROWS, WIDTH), F32)...  180 us

profile of v4, /device:TPU:30, one launch (start us, length us, event | category | flops | bytes accessed | tf_op | source)
XLA Modules:
  0.0 183.5 jit_solution(14019103295466540552)
XLA Ops:
  0.7 179.7 %shard_map.73 = f32[256,2048]{1,0:T(8,128)} custom-call(s32[32]{0:T(128)} %partner_ref.1, s32[16,16]{1,0:T(8,128)} %mask_ref.1, f32[1]{0:T(128)S(6)} %copy.9.pair_ref, f32[256,2048]{1,0:T(8,128)} %bitcast.5, f32[256,2048]{1,0:T(8,128)} %bitcast.6, f32[256,2048]{1,0:T(8,128)} %op_hbm.1, f32[1,2048]{1,0:T(1,128)} %bitcast.7), custom_call_target="tpu_custom_call" | custom-call | tf_op jit(solution)/shard_map/pallas_call | solution.py:489
  180.4 3.1 %copy.10 = f32[1,256,2048]{2,1,0:T(8,128)} copy(f32[1,256,2048]{2,1,0:T(8,128)} %bitcast.4) | data formatting | bytes 4194304

commit v5 on v4

--- a/solution.py
+++ b/solution.py
@@ -366,6 +366,28 @@
         turned[c][p] = spread[sweep][c][partner_ref[p]]
         pltpu.make_async_copy(turned[c].at[p], mirror[sweep][c].at[p], hop_in.at[number]).start()
 
+    def combine(sweep, chunk):
+        number = sweep * 8 + 4 + chunk
+        pltpu.make_async_copy(mirror[sweep][chunk], mirror[sweep][chunk], hop_in.at[number]).wait()
+        for (j, h), (c, plane) in PIECES.items():
+            if c != chunk:
+                continue
+
+            def one(core_of, carry, j=j, h=h, plane=plane):
+                lanes = columns_of(j, core_of, h)
+                place = pl.ds(pl.multiple_of(core_of * BLOCK, BLOCK), BLOCK)
+                other = mirror[sweep][chunk][plane * PLANE:(plane + 1) * PLANE, :, place]
+                below = side[...] + virt_ref[:, lanes] + pair_ref[0]
+                value = (ints[:, lanes] + prods[sweep][:, lanes] + other.reshape(ROWS, BLOCK)) / below
+                if sweep == ITERS - 1:
+                    out_ref[:, lanes] = value
+                else:
+                    depth = depth_of(j, core_of, h)
+                    a_high[:, depth], a_low[:, depth] = split(value)
+                return carry
+
+            lax.fori_loop(0, 2, one, 0)
+
     def exchange(sweep, first, count):
         multiply(prods[sweep], first, count, z_hi, True)
         flip(sweep, 0)
@@ -380,29 +402,11 @@
         flip(sweep, 3)
         give(sweep, 1, 3)
         give(sweep, 2)
+        combine(sweep, 0)
+        combine(sweep, 1)
+        if sweep == 0:
+            multiply_all(prods[1], 0, 4, False)
         give(sweep, 3)
-
-    def combine(sweep, chunk):
-        number = sweep * 8 + 4 + chunk
-        pltpu.make_async_copy(mirror[sweep][chunk], mirror[sweep][chunk], hop_in.at[number]).wait()
-        for (j, h), (c, plane) in PIECES.items():
-            if c != chunk:
-                continue
-
-            def one(core_of, carry, j=j, h=h, plane=plane):
-                lanes = columns_of(j, core_of, h)
-                place = pl.ds(pl.multiple_of(core_of * BLOCK, BLOCK), BLOCK)
-                other = mirror[sweep][chunk][plane * PLANE:(plane + 1) * PLANE, :, place]
-                below = side[...] + virt_ref[:, lanes] + pair_ref[0]
-                value = (ints[:, lanes] + prods[sweep][:, lanes] + other.reshape(ROWS, BLOCK)) / below
-                if sweep == ITERS - 1:
-                    out_ref[:, lanes] = value
-                else:
-                    depth = depth_of(j, core_of, h)
-                    a_high[:, depth], a_low[:, depth] = split(value)
-                return carry
-
-            lax.fori_loop(0, 2, one, 0)
 
     def drain(sweep):
         sent = turned_in[0].at[pl.ds(0, 3)]
@@ -463,15 +467,12 @@
         use(unit)
     loads[-1].wait()
     exchange(0, ORDER[FAR[1]], 1)
-    combine(0, 0)
-    combine(0, 1)
-    multiply_all(prods[1], 0, 4, False)
     combine(0, 2)
     multiply_all(prods[1], 4, 2, True)
     combine(0, 3)
     drain(0)
     exchange(1, 6, 2)
-    for c in range(CHUNKS):
+    for c in (2, 3):
         combine(1, c)
     drain(1)
     for copy in everything:

time: 187 us -> 188 us (level)
  no operation moved by 1% of the time
where the time goes in v5:
time: 188 us; the launch traced here: 185 us
  Pallas kernels  181 us (96%)
  local copies, waits for them, and re-layouts  3.14 us (2%)
    pallas_call x1, Pallas kernels, per_device(): pl.pallas_call(kernel, out_shape=jax.ShapeDtypeStruct((ROWS, WIDTH), F32)...  181 us

profile of v5, /device:TPU:30, one launch (start us, length us, event | category | flops | bytes accessed | tf_op | source)
XLA Modules:
  0.0 185.3 jit_solution(2430553835210392748)
XLA Ops:
  0.7 181.5 %shard_map.73 = f32[256,2048]{1,0:T(8,128)} custom-call(s32[32]{0:T(128)} %partner_ref.1, s32[16,16]{1,0:T(8,128)} %mask_ref.1, f32[1]{0:T(128)S(6)} %copy.9.pair_ref, f32[256,2048]{1,0:T(8,128)} %bitcast.5, f32[256,2048]{1,0:T(8,128)} %bitcast.6, f32[256,2048]{1,0:T(8,128)} %op_hbm.1, f32[1,2048]{1,0:T(1,128)} %bitcast.7), custom_call_target="tpu_custom_call" | custom-call | tf_op jit(solution)/shard_map/pallas_call | solution.py:490
  182.1 3.1 %copy.10 = f32[1,256,2048]{2,1,0:T(8,128)} copy(f32[1,256,2048]{2,1,0:T(8,128)} %bitcast.4) | data formatting | bytes 4194304
